TPU v7x, 512 devices: a whole 4x4x16 slice. The times are simulated.
512 devices in a mesh: replica: 32 (over z, y_hi), tensor: 16 (over y_lo, x, core).
Axes of the slice: x: 4, y: 4 (y_hi: 2, y_lo: 2; y = y_hi * 2 + y_lo), z: 16, core: 2. Of those that a mesh axis runs over, the one named last changes fastest.
Arguments:
- key_head_weight: bfloat16 [16, 128, 8192], P('tensor'), may hold values from -6 to 6
- down_factor_slots: float32 [32, 2, 8192], P('replica', None, 'tensor'), may hold values from -6 to 6
- adapter_up_factor: float32 [64, 1024], P('replica'), may hold values from -0.2 to 0.2
- piece_slot_index: int32 [32], replicated, may hold values from 0 to 31, each once
Outputs:
- merged: bfloat16 [16, 128, 8192], P('tensor')
Inputs may be any that keep to these rules, and one draw needn't show every extreme that they name: Piece p lies in slot piece_slot_index[p] of down_factor_slots; every slot holds exactly one piece.
All inputs are finite; a program needn't handle non-finite values.
Results may differ from a plain program's by a relative error of at most 0.001.
Values sent between devices are 32-bit elements; how exact they have to be, the bound alone decides.
A program may use at most 64 MiB of HBM per device.

v0:
```python
import jax
import jax.numpy as jnp
from jax import lax
from jax.sharding import PartitionSpec as P

KV_HEADS = 8
merge_scale = 2.0


def arrange_pieces(slot_row_count, piece_slot_index, factor_rank):
    ordered = jnp.take(slot_row_count, piece_slot_index, axis=0)
    return ordered.reshape(factor_rank, ordered.shape[-1])


def merge_weight_block(resident_block, down_factor_rows, adapter_rows):
    lowrank_update = jnp.dot(
        adapter_rows.T,
        down_factor_rows,
        preferred_element_type=jnp.float32,
        precision=lax.Precision.HIGHEST,
    )
    return (resident_block.astype(jnp.float32) + merge_scale * lowrank_update[None]).astype(
        jnp.bfloat16
    )


def local(key_head_weight, down_factor_slots, adapter_up_factor, piece_slot_index):
    output_units = key_head_weight.shape[1]
    copies = max(1, lax.axis_size("tensor") // KV_HEADS)
    first_index = lax.axis_index("tensor") // copies * output_units
    adapter_columns = lax.dynamic_slice_in_dim(adapter_up_factor, first_index, output_units, 1)
    owner_rows = lax.all_gather(down_factor_slots, "tensor", axis=2, tiled=True)
    slot_row_count, adapter_rows = (
        lax.all_gather(owner_rows, "replica", axis=0, tiled=True),
        lax.all_gather(adapter_columns, "replica", axis=0, tiled=True),
    )
    down_factor_rows = arrange_pieces(slot_row_count, piece_slot_index, adapter_rows.shape[0])
    return merge_weight_block(key_head_weight, down_factor_rows, adapter_rows)


def solution(mesh):
    in_specs = (P("tensor", None, None), P("replica", None, "tensor"), P("replica", None), P())
    out_specs = P("tensor", None, None)
    return jax.shard_map(local, mesh=mesh, in_specs=in_specs, out_specs=out_specs, check_vma=False)
```

profile of v0, /device:TPU:2, one launch (start us, length us, event | category | flops | bytes accessed | tf_op | source)
XLA Modules:
  0.0 201.6 jit_solution(13053699690656250366)
XLA Ops:
  6.5 0.0 copy-start
  6.5 0.0 all-gather.3.cloned.1.call-start
  6.5 23.7 %all_gather.10 = f32[1,2,8192]{2,1,0:T(2,128)} all-gather(f32[1,2,512]{2,1,0:T(2,128)} %param.5), channel_id=1, replica_groups=mesh['replica'=32,'tensor'=16] {'tensor'}, dimensions={2}, use_global_device_ids=true | all-gather | bytes 69632 | tf_op jit(solution)/shard_map/all_gather | solution.py:32
  30.3 0.0 all-gather.3.cloned.1.call-update
  30.3 0.7 compare_and_fusion
  31.0 0.1 broadcast_in_dim.17
  31.0 0.1 broadcast_in_dim.18
  31.2 0.0 copy-done
  31.2 77.4 %all-gather = f32[32,2,128]{2,1,0:T(2,128)S(1)} all-gather(f32[1,2,128]{2,1,0:T(2,128)S(1)} %dynamic-slice_bitcast_fusion), channel_id=1, replica_groups=mesh['replica'=32,'tensor'=16] {'replica'}, dimensions={0}, use_global_device_ids=true | all-gather | bytes 33792 | tf_op jit(solution)/shard_map/all_gather | solution.py:35
  108.6 0.7 compare_select_fusion
  109.2 70.9 %all-gather.3.cloned.1.call-done = f32[32,2,8192]{2,1,0:T(2,128)} async-done(((f32[1,2,8192]{2,1,0:T(2,128)}), f32[32,2,8192]{2,1,0:T(2,128)}) %all-gather.3.cloned.1.call-update) | async-done | bytes 2097168 | tf_op jit(solution)/shard_map/all_gather | solution.py:34
  180.2 5.6 %gather_fusion = f32[32,2,8192]{2,1,0:T(2,128)} fusion(f32[32,2,8192]{2,1,0:T(2,128)} %all-gather.3.cloned.1.call-done, s32[1024]{0:T(1024)S(1)} %pad_clamp_fusion), kind=kCustom, calls=%fused_computation | custom fusion | bytes 4194432 | tf_op jit(solution)/shard_map/jit(_take)/gather | solution.py:11
  185.7 2.7 %gather.7 = f32[64,8192]{1,0:T(8,128)S(1)} reshape(f32[32,2,8192]{2,1,0:T(2,128)} %gather_fusion) | data formatting | bytes 4194304 | tf_op jit(solution)/shard_map/jit(_take)/gather | solution.py:11
  188.4 6.4 %fusion.2 = bf16[1,128,8192]{2,1,0:T(8,128)(2,1)} fusion(f32[64,128]{1,0:T(8,128)S(1)} %bitcast.10, bf16[1,128,8192]{2,1,0:T(8,128)(2,1)} %param.4, f32[64,8192]{1,0:T(8,128)S(1)} %gather.7, pred[64]{0:T(512)(128)(4,1)S(1)} %broadcast_in_dim.18), kind=kOutput, calls=%fused_computation.4 | convolution fusion | flops 810024960 | bytes 6324288 | tf_op jit(solution)/shard_map/dot_general | solution.py:16
  (2 shorter events, 0.0 us)
Async XLA Ops:
  6.5 24.6 %copy-start = (f32[2,1024]{1,0:T(2,128)S(1)}, f32[2,1024]{1,0:T(2,128)}, u32[]{:S(2)}) copy-start(f32[2,1024]{1,0:T(2,128)} %param.6) | copy-start | bytes 24580
  6.5 173.6 %all-gather.3.cloned.1.call-start = ((), (), s32[]{:S(2)}) async-start(), calls=%async_computation | async-start | bytes 2162688 | tf_op jit(solution)/shard_map/all_gather | solution.py:34
Sparse Core Ops, SparseCore 0:
  30.4 149.7 all-gather.2
where the time goes:
time: 202 us
  blocking collectives  101 us (50%)
  waiting for transfers between devices  70.9 us (35%)
  between operations  13.4 us (7%)
  local copies, waits for them, and re-layouts  8.46 us (4%)
  matrix products  6.37 us (3%)
    all_gather x1, blocking collectives, local(): lax.all_gather(adapter_columns, 'replica', axis=0, tiled=True)  77.4 us
    all_gather x1, waiting for transfers between devices, local(): lax.all_gather(owner_rows, 'replica', axis=0, tiled=True)  70.9 us
    all_gather x1, blocking collectives, local(): owner_rows = lax.all_gather(down_factor_slots, 'tensor', axis=2, tiled=True)  23.7 us
    gather x2, local copies, waits for them, and re-layouts, arrange_pieces(): ordered = jnp.take(slot_row_count, piece_slot_index, axis=0)  8.26 us
    dot_general x1, matrix products, merge_weight_block(): jnp.dot(adapter_rows.T, down_factor_rows, preferred_element_type=jnp.floa...  6.37 us
  transfers between devices with their start and end apart: 1, of which 1 were waited for; matrix products, arithmetic and copies ran while one was open for 1% of the time, Pallas kernels for 0%

commit v1 on v0

--- a/solution.py
+++ b/solution.py
@@ -29,7 +29,10 @@
     copies = max(1, lax.axis_size("tensor") // KV_HEADS)
     first_index = lax.axis_index("tensor") // copies * output_units
     adapter_columns = lax.dynamic_slice_in_dim(adapter_up_factor, first_index, output_units, 1)
-    owner_rows = lax.all_gather(down_factor_slots, "tensor", axis=2, tiled=True)
+    n_dev = lax.axis_size("tensor")
+    pieces = jnp.stack([down_factor_slots for _ in range(n_dev)])
+    pieces = lax.all_to_all(pieces, "tensor", split_axis=0, concat_axis=0)
+    owner_rows = jnp.concatenate(pieces, axis=2)
     slot_row_count, adapter_rows = (
         lax.all_gather(owner_rows, "replica", axis=0, tiled=True),
         lax.all_gather(adapter_columns, "replica", axis=0, tiled=True),

time: 202 us -> 193 us (0.955)
  blocking collectives: 101 us -> 92.8 us
    all_gather x1 -> x0, blocking collectives: 23.7 us -> none  [local(): owner_rows = lax.all_gather(down_factor_slots, 'tensor', axis=2, tiled=True)]
    all_to_all x0 -> x1, blocking collectives: none -> 13.8 us  [local(): pieces = lax.all_to_all(pieces, 'tensor', split_axis=0, concat_axis=0)]
where the time goes in v1:
time: 193 us
  blocking collectives  92.8 us (48%)
  waiting for transfers between devices  69.8 us (36%)
  between operations  13.4 us (7%)
  local copies, waits for them, and re-layouts  9.17 us (5%)
  matrix products  6.37 us (3%)
    all_gather x1, blocking collectives, local(): lax.all_gather(adapter_columns, 'replica', axis=0, tiled=True)  79 us
    all_gather x1, waiting for transfers between devices, local(): lax.all_gather(owner_rows, 'replica', axis=0, tiled=True)  69.8 us
    all_to_all x1, blocking collectives, local(): pieces = lax.all_to_all(pieces, 'tensor', split_axis=0, concat_axis=0)  13.8 us
    gather x2, local copies, waits for them, and re-layouts, arrange_pieces(): ordered = jnp.take(slot_row_count, piece_slot_index, axis=0)  8.26 us
    dot_general x1, matrix products, merge_weight_block(): jnp.dot(adapter_rows.T, down_factor_rows, preferred_element_type=jnp.floa...  6.37 us
  transfers between devices with their start and end apart: 1, of which 1 were waited for; matrix products, arithmetic and copies ran while one was open for 1% of the time, Pallas kernels for 0%

profile of v1, /device:TPU:2, one launch (start us, length us, event | category | flops | bytes accessed | tf_op | source)
XLA Modules:
  0.0 192.9 jit_solution(11286800726962515689)
XLA Ops:
  6.5 0.0 copy-start
  6.5 0.0 all-gather.3.cloned.1.call-start
  6.5 0.7 stack.2
  7.3 13.8 %all_to_all.5 = f32[16,1,2,512]{3,2,1,0:T(2,128)} all-to-all(f32[16,1,2,512]{3,2,1,0:T(2,128)S(1)} %stack.2), channel_id=1, replica_groups=mesh['replica'=32,'tensor'=16] {'tensor'}, dimensions={0} | all-to-all | bytes 131072 | tf_op jit(solution)/shard_map/all_to_all | solution.py:34
  21.1 0.0 all-gather.3.cloned.1.call-update
  21.1 0.7 compare_and_fusion
  21.8 0.1 broadcast_in_dim.17
  21.9 0.1 broadcast_in_dim.18
  22.0 0.0 copy-done
  22.0 79.0 %all-gather = f32[32,2,128]{2,1,0:T(2,128)S(1)} all-gather(f32[1,2,128]{2,1,0:T(2,128)S(1)} %dynamic-slice_bitcast_fusion), channel_id=1, replica_groups=mesh['replica'=32,'tensor'=16] {'replica'}, dimensions={0}, use_global_device_ids=true | all-gather | bytes 33792 | tf_op jit(solution)/shard_map/all_gather | solution.py:38
  101.0 0.7 compare_select_fusion
  101.7 69.8 %all-gather.3.cloned.1.call-done = f32[32,2,8192]{2,1,0:T(2,128)} async-done(((f32[1,2,8192]{2,1,0:T(2,128)}), f32[32,2,8192]{2,1,0:T(2,128)}) %all-gather.3.cloned.1.call-update) | async-done | bytes 2097168 | tf_op jit(solution)/shard_map/all_gather | solution.py:37
  171.4 5.6 %gather_fusion = f32[32,2,8192]{2,1,0:T(2,128)} fusion(f32[32,2,8192]{2,1,0:T(2,128)} %all-gather.3.cloned.1.call-done, s32[1024]{0:T(1024)S(1)} %pad_clamp_fusion), kind=kCustom, calls=%fused_computation | custom fusion | bytes 4194432 | tf_op jit(solution)/shard_map/jit(_take)/gather | solution.py:11
  177.0 2.7 %gather.7 = f32[64,8192]{1,0:T(8,128)S(1)} reshape(f32[32,2,8192]{2,1,0:T(2,128)} %gather_fusion) | data formatting | bytes 4194304 | tf_op jit(solution)/shard_map/jit(_take)/gather | solution.py:11
  179.7 6.4 %fusion.2 = bf16[1,128,8192]{2,1,0:T(8,128)(2,1)} fusion(f32[64,128]{1,0:T(8,128)S(1)} %bitcast.15, bf16[1,128,8192]{2,1,0:T(8,128)(2,1)} %param.4, f32[64,8192]{1,0:T(8,128)S(1)} %gather.7, pred[64]{0:T(512)(128)(4,1)S(1)} %broadcast_in_dim.18), kind=kOutput, calls=%fused_computation.4 | convolution fusion | flops 810024960 | bytes 6324288 | tf_op jit(solution)/shard_map/dot_general | solution.py:16
  (2 shorter events, 0.0 us)
Async XLA Ops:
  6.5 15.5 %copy-start = (f32[2,1024]{1,0:T(2,128)S(1)}, f32[2,1024]{1,0:T(2,128)}, u32[]{:S(2)}) copy-start(f32[2,1024]{1,0:T(2,128)} %param.6) | copy-start | bytes 24580
  6.5 164.9 %all-gather.3.cloned.1.call-start = ((), (), s32[]{:S(2)}) async-start(), calls=%async_computation.1 | async-start | bytes 2162688 | tf_op jit(solution)/shard_map/all_gather | solution.py:37
Sparse Core Ops, SparseCore 0:
  21.2 150.1 all-gather.2
